TPU v7x, 32 devices: a whole 2x2x4 slice. The times are simulated.
32 devices in a mesh: section: 4 (over z), ctx: 4 (over x, core), dp: 2 (over y).
Axes of the slice: x: 2, y: 2, z: 4, core: 2. Of those that a mesh axis runs over, the one named last changes fastest.
Arguments:
- stream: bfloat16 [4, 256, 8192], P('section', 'dp', 'ctx'), may hold values from -6 to 6
- norm_gain: float32 [4, 8192], P('section', 'ctx'), may hold values from 0.5 to 2
- w_router: bfloat16 [4, 8192], P('section', 'ctx'), may hold values from -0.0625 to 0.0625
- w_gate: bfloat16 [4, 8192, 14336], P('section', 'ctx', 'dp'), may hold values from -0.0625 to 0.0625
- w_up: bfloat16 [4, 8192, 14336], P('section', 'ctx', 'dp'), may hold values from -0.0625 to 0.0625
- w_down: bfloat16 [4, 14336, 8192], P('section', 'dp', 'ctx'), may hold values from -0.046875 to 0.046875
- keep_rows: int32 [2, 4, 2, 32], P(None, 'section', 'dp'), may hold values from -1 to 127, as said below
Outputs:
- advanced: bfloat16 [4, 256, 8192], P('section', 'dp', 'ctx')
Inputs may be any that keep to these rules, and one draw needn't show every extreme that they name: `keep_rows`: each list holds distinct row indices first, then -1 in its empty slots. Over the 2 lists of one tick and section exactly 32 rows are kept; in each tick and section some list is full and some is empty.
All inputs are finite; a program needn't handle non-finite values.
Results may differ from a plain program's by a relative error of at most 0.005.
Values may be sent and summed in bfloat16 or wider, within the bound.
A program may use at most 192 MiB of HBM per device.

v0:
```python
import jax
import jax.numpy as jnp
from jax import lax
from jax.sharding import PartitionSpec as P

D = 8192
eps = 1e-05


def from_behind(value, axis, steps):
    count = lax.axis_size(axis)
    pairs = [(source, (source + steps) % count) for source in range(count)]
    return lax.ppermute(value, axis, pairs)


def hidden_block(normed, w_gate, w_up, w_down):
    row_piece = lax.all_gather(normed, "dp", axis=0, tiled=True)
    gate_part = jnp.dot(row_piece, w_gate, preferred_element_type=jnp.float32)
    up_part = jnp.dot(row_piece, w_up, preferred_element_type=jnp.float32)
    partial_value = jnp.stack([gate_part, up_part], axis=1)
    summed = lax.psum(partial_value, "ctx")
    hidden = (jax.nn.silu(summed[:, 0]) * summed[:, 1]).astype(jnp.bfloat16)
    return lax.psum_scatter(
        jnp.dot(hidden, w_down, preferred_element_type=jnp.float32).astype(jnp.bfloat16),
        "dp",
        scatter_dimension=0,
        tiled=True,
    ).astype(jnp.float32)


def routed_layer(stream, keep_list, gain_row, router, w_gate, w_up, w_down):
    is_kept = keep_list >= 0
    picked = jnp.take(stream, jnp.maximum(keep_list, 0), axis=0)
    rows_wide = picked.astype(jnp.float32)
    squares = jnp.sum(rows_wide * rows_wide, axis=1)
    logits = jnp.sum(rows_wide * router.astype(jnp.float32)[None, :], axis=1)
    squares, logits = lax.psum((squares, logits), "ctx")
    scaling = lax.rsqrt(squares / D + eps)
    normed = jnp.where(
        is_kept[:, None], rows_wide * scaling[:, None] * gain_row[None, :], 0.0
    ).astype(jnp.bfloat16)
    update = hidden_block(normed, w_gate, w_up, w_down)
    new_rows = (rows_wide + jax.nn.sigmoid(logits)[:, None] * update).astype(jnp.bfloat16)
    target = jnp.where(is_kept, keep_list, stream.shape[0])
    return stream.at[target].set(new_rows, mode="drop")


def local(stream, norm_gain, w_router, w_gate, w_up, w_down, keep_rows):
    first_pass = routed_layer(
        stream[0], keep_rows[0, 0, 0], norm_gain[0], w_router[0], w_gate[0], w_up[0], w_down[0]
    )
    passed = from_behind(first_pass, "section", 1)
    second_pass = routed_layer(
        passed, keep_rows[1, 0, 0], norm_gain[0], w_router[0], w_gate[0], w_up[0], w_down[0]
    )
    section_place = lax.axis_index("section")
    result = jnp.where(section_place == 0, passed, second_pass)
    return result[None]


def solution(mesh):
    return jax.shard_map(
        local,
        mesh=mesh,
        in_specs=(
            P("section", "dp", "ctx"),
            P("section", "ctx"),
            P("section", "ctx"),
            P("section", "ctx", "dp"),
            P("section", "ctx", "dp"),
            P("section", "dp", "ctx"),
            P(None, "section", "dp", None),
        ),
        out_specs=P("section", "dp", "ctx"),
        check_vma=False,
    )
```

profile of v0, /device:TPU:0, one launch (start us, length us, event | category | flops | bytes accessed | tf_op | source)
XLA Modules:
  0.0 325.9 jit_solution(13672440571319732338)
XLA Ops:
  6.5 0.0 all-reduce.5.cloned.1.call-start
  6.5 1.0 copy.13
  7.6 0.7 compare_and_fusion
  8.3 0.7 compare_bitcast_fusion
  8.9 0.7 mul.113
  9.7 0.7 gather_fusion
  10.3 0.2 fusion.36
  10.5 8.3 %all-reduce.1 = (f32[32]{0:T(128)S(1)}, f32[32]{0:T(128)S(1)}) all-reduce(f32[32]{0:T(128)S(1)} %get-tuple-element.9, f32[32]{0:T(128)S(1)} %get-tuple-element.8), channel_id=1, replica_groups=mesh['section'=4,'ctx'=4,'dp'=2] {'ctx'}, use_global_device_ids=true, to_apply=%region_3.5 | all-reduce | flops 64 | bytes 512 | tf_op jit(solution)/shard_map/psum | solution.py:37
  18.9 0.8 fusion.40
  19.7 5.6 %all_gather.6 = bf16[64,2048]{1,0:T(8,128)(2,1)S(1)} all-gather(bf16[32,2048]{1,0:T(8,128)(2,1)S(1)} %fusion.40), channel_id=1, replica_groups=mesh['section'=4,'ctx'=4,'dp'=2] {'dp'}, dimensions={0}, use_global_device_ids=true | all-gather | bytes 393216 | tf_op jit(solution)/shard_map/all_gather | solution.py:17
  25.4 12.0 %fusion.12 = f32[64,1,7168]{2,0,1:T(8,128)S(1)} fusion(bf16[64,2048]{1,0:T(8,128)(2,1)S(1)} %all_gather.6, bf16[1,2048,7168]{2,1,0:T(8,128)(2,1)} %param.12), kind=kOutput, calls=%fused_computation.16 | convolution fusion | flops 1879048192 | bytes 31457280 | tf_op jit(solution)/shard_map/dot_general | solution.py:18
  37.3 12.0 %fusion.18 = f32[64,1,7168]{2,0,1:T(8,128)S(1)} fusion(bf16[64,2048]{1,0:T(8,128)(2,1)S(1)} %all_gather.6, bf16[1,2048,7168]{2,1,0:T(8,128)(2,1)} %param.13), kind=kOutput, calls=%fused_computation.18 | convolution fusion | flops 1879048192 | bytes 31457280 | tf_op jit(solution)/shard_map/dot_general | solution.py:19
  49.3 2.1 pad_maximum_fusion
  51.4 0.0 all-reduce.5.cloned.1.call-update
  51.5 0.0 copy-start.1
  51.5 0.0 copy-start
  51.5 0.0 reduce-scatter.3.cloned.1.call-start
  51.5 77.4 %all-reduce.5.cloned.1.call-done = f32[64,2,7168]{2,0,1:T(8,128)} async-done(((f32[64,2,7168]{2,0,1:T(8,128)}), f32[64,2,7168]{2,0,1:T(8,128)}) %all-reduce.5.cloned.1.call-update) | async-done | bytes 3670032 | tf_op jit(solution)/shard_map/psum | solution.py:21
  128.9 16.4 %fusion.24 = bf16[64,2048]{1,0:T(8,128)(2,1)} fusion(bf16[1,7168,2048]{2,1,0:T(8,128)(2,1)} %param.14, f32[64,2,7168]{2,0,1:T(8,128)} %all-reduce.5.cloned.1.call-done), kind=kOutput, calls=%fused_computation.22 | convolution fusion | flops 1881931776 | bytes 33292288 | tf_op jit(solution)/shard_map/dot_general | solution.py:24
  145.3 0.0 reduce-scatter.3.cloned.1.call-update
  145.3 0.0 all-reduce.7.cloned.1.call-start
  145.4 0.0 copy-done.1
  145.4 11.9 %reduce-scatter.3.cloned.1.call-done = bf16[32,2048]{1,0:T(8,128)(2,1)} async-done(((bf16[64,2048]{1,0:T(8,128)(2,1)}), bf16[32,2048]{1,0:T(8,128)(2,1)}) %reduce-scatter.3.cloned.1.call-update) | async-done | bytes 131088 | tf_op jit(solution)/shard_map/reduce_scatter | solution.py:23
  157.3 1.6 scatter_custom_fusion
  158.9 1.5 collective-permute-start
  160.4 14.0 %collective-permute-done = bf16[128,2048]{1,0:T(8,128)(2,1)S(1)} collective-permute-done((bf16[128,2048]{1,0:T(8,128)(2,1)S(1)}, bf16[128,2048]{1,0:T(8,128)(2,1)S(1)}, u32[]{:S(2)}, u32[]{:S(2)}) %collective-permute-start) | collective-permute-done | bytes 524320 | tf_op jit(solution)/shard_map/ppermute | solution.py:13
  174.4 0.6 gather_fusion.1
  175.0 0.2 fusion.42
  175.3 5.7 %all-reduce = (f32[32]{0:T(128)S(1)}, f32[32]{0:T(128)S(1)}) all-reduce(f32[32]{0:T(128)S(1)} %get-tuple-element.7, f32[32]{0:T(128)S(1)} %get-tuple-element.6), channel_id=1, replica_groups=mesh['section'=4,'ctx'=4,'dp'=2] {'ctx'}, use_global_device_ids=true, to_apply=%region_10.12 | all-reduce | flops 64 | bytes 512 | tf_op jit(solution)/shard_map/psum | solution.py:37
  181.0 0.0 copy-done
  181.0 0.1 fusion.46
  181.1 6.1 %all_gather.7 = bf16[64,2048]{1,0:T(8,128)(2,1)S(1)} all-gather(bf16[32,2048]{1,0:T(8,128)(2,1)S(1)} %fusion.46), channel_id=1, replica_groups=mesh['section'=4,'ctx'=4,'dp'=2] {'dp'}, dimensions={0}, use_global_device_ids=true | all-gather | bytes 393216 | tf_op jit(solution)/shard_map/all_gather | solution.py:17
  187.2 12.0 %fusion.15 = f32[64,1,7168]{2,0,1:T(8,128)S(1)} fusion(bf16[64,2048]{1,0:T(8,128)(2,1)S(1)} %all_gather.7, bf16[1,2048,7168]{2,1,0:T(8,128)(2,1)} %param.12), kind=kOutput, calls=%fused_computation.17 | convolution fusion | flops 1879048192 | bytes 31457280 | tf_op jit(solution)/shard_map/dot_general | solution.py:18
  199.2 12.0 %fusion.21 = f32[64,1,7168]{2,0,1:T(8,128)S(1)} fusion(bf16[64,2048]{1,0:T(8,128)(2,1)S(1)} %all_gather.7, bf16[1,2048,7168]{2,1,0:T(8,128)(2,1)} %param.13), kind=kOutput, calls=%fused_computation.19 | convolution fusion | flops 1879048192 | bytes 31457280 | tf_op jit(solution)/shard_map/dot_general | solution.py:19
  211.2 2.1 pad_maximum_fusion.1
  213.3 0.0 all-reduce.7.cloned.1.call-update
  213.3 0.0 reduce-scatter.5.cloned.1.call-start
  213.4 75.2 %all-reduce.7.cloned.1.call-done = f32[64,2,7168]{2,0,1:T(8,128)} async-done(((f32[64,2,7168]{2,0,1:T(8,128)}), f32[64,2,7168]{2,0,1:T(8,128)}) %all-reduce.7.cloned.1.call-update) | async-done | bytes 3670032 | tf_op jit(solution)/shard_map/psum | solution.py:21
  288.6 16.4 %fusion.27 = bf16[64,2048]{1,0:T(8,128)(2,1)} fusion(bf16[1,7168,2048]{2,1,0:T(8,128)(2,1)} %param.14, f32[64,2,7168]{2,0,1:T(8,128)} %all-reduce.7.cloned.1.call-done), kind=kOutput, calls=%fused_computation.23 | convolution fusion | flops 1881931776 | bytes 33292288 | tf_op jit(solution)/shard_map/dot_general | solution.py:24
  305.0 0.0 reduce-scatter.5.cloned.1.call-update
  305.1 11.9 %reduce-scatter.5.cloned.1.call-done = bf16[32,2048]{1,0:T(8,128)(2,1)} async-done(((bf16[64,2048]{1,0:T(8,128)(2,1)}), bf16[32,2048]{1,0:T(8,128)(2,1)}) %reduce-scatter.5.cloned.1.call-update) | async-done | bytes 131088 | tf_op jit(solution)/shard_map/reduce_scatter | solution.py:23
  316.9 1.6 scatter_custom_fusion.1
  318.5 0.9 select_bitcast_fusion
  (8 shorter events, 0.1 us)
Async XLA Ops:
  6.5 122.4 %all-reduce.5.cloned.1.call-start = ((), (), s32[]{:S(2)}) async-start(), calls=%async_computation.2 | async-start | bytes 7340032 | tf_op jit(solution)/shard_map/psum | solution.py:21
  51.5 93.9 %copy-start.1 = (s32[2,1,1,32]{3,2,1,0:T(1,128)S(1)}, s32[2,1,1,32]{3,2,1,0:T(1,128)}, u32[]{:S(2)}) copy-start(s32[2,1,1,32]{3,2,1,0:T(1,128)} %param.15) | copy-start | bytes 772
  51.5 129.5 %copy-start = (f32[1,2048]{1,0:T(1,128)S(1)}, f32[1,2048]{1,0:T(1,128)}, u32[]{:S(2)}) copy-start(f32[1,2048]{1,0:T(1,128)} %param.10) | copy-start | bytes 24580
  51.5 105.8 %reduce-scatter.3.cloned.1.call-start = ((), (), s32[]{:S(2)}) async-start(), calls=%async_computation.3 | async-start | bytes 393216 | tf_op jit(solution)/shard_map/reduce_scatter | solution.py:23
  145.3 143.3 %all-reduce.7.cloned.1.call-start = ((), (), s32[]{:S(2)}) async-start(), calls=%async_computation.4 | async-start | bytes 7340032 | tf_op jit(solution)/shard_map/psum | solution.py:21
  158.9 15.5 %collective-permute-start = (bf16[128,2048]{1,0:T(8,128)(2,1)S(1)}, bf16[128,2048]{1,0:T(8,128)(2,1)S(1)}, u32[]{:S(2)}, u32[]{:S(2)}) collective-permute-start(bf16[128,2048]{1,0:T(8,128)(2,1)S(1)} %scatter_custom_fusion), channel_id=1, source_target_pairs={{0,8},{8,16},{16,24},{24,0},{1,9},{9,17},{17,25},{25,1},{2,10},{10... | collective-permute-start | bytes 1572872 | tf_op jit(solution)/shard_map/ppermute | solution.py:13
  213.3 103.6 %reduce-scatter.5.cloned.1.call-start = ((), (), s32[]{:S(2)}) async-start(), calls=%async_computation.5 | async-start | bytes 393216 | tf_op jit(solution)/shard_map/reduce_scatter | solution.py:23
Sparse Core Ops, SparseCore 0:
  51.6 77.3 all-reduce.4
  145.5 11.7 reduce-scatter.2
  213.4 75.1 all-reduce.6
  305.1 11.7 reduce-scatter.4
where the time goes:
time: 326 us
  waiting for transfers between devices  190 us (58%)
  matrix products  80.7 us (25%)
  blocking collectives  25.8 us (8%)
  between operations  13.3 us (4%)
  other arithmetic  11.7 us (4%)
    psum x2, waiting for transfers between devices, hidden_block(): summed = lax.psum(partial_value, 'ctx')  153 us
    dot_general x2, matrix products, hidden_block(): jnp.dot(hidden, w_down, preferred_element_type=jnp.float32)  32.8 us
    dot_general x2, matrix products, hidden_block(): up_part = jnp.dot(row_piece, w_up, preferred_element_type=jnp.float32)  24 us
    dot_general x2, matrix products, hidden_block(): gate_part = jnp.dot(row_piece, w_gate, preferred_element_type=jnp.float32)  24 us
    reduce_scatter x2, waiting for transfers between devices, hidden_block(): lax.psum_scatter(jnp.dot(hidden, w_down, preferred_element_type=jnp.float...  23.7 us
    psum x2, blocking collectives, routed_layer(): squares, logits = lax.psum((squares, logits), 'ctx')  14 us
    ppermute x1, waiting for transfers between devices, from_behind(): return lax.ppermute(value, axis, pairs)  14 us
    all_gather x2, blocking collectives, hidden_block(): row_piece = lax.all_gather(normed, 'dp', axis=0, tiled=True)  11.7 us
  transfers between devices with their start and end apart: 5, of which 5 were waited for; matrix products, arithmetic and copies ran while one was open for 0% of the time, Pallas kernels for 0%

commit v1 on v0

--- a/solution.py
+++ b/solution.py
@@ -18,7 +18,9 @@
     gate_part = jnp.dot(row_piece, w_gate, preferred_element_type=jnp.float32)
     up_part = jnp.dot(row_piece, w_up, preferred_element_type=jnp.float32)
     partial_value = jnp.stack([gate_part, up_part], axis=1)
-    summed = lax.psum(partial_value, "ctx")
+    summed = partial_value
+    for hop in (1, 2):
+        summed = summed + lax.ppermute(summed, "ctx", [(dev, dev ^ hop) for dev in range(4)])
     hidden = (jax.nn.silu(summed[:, 0]) * summed[:, 1]).astype(jnp.bfloat16)
     return lax.psum_scatter(
         jnp.dot(hidden, w_down, preferred_element_type=jnp.float32).astype(jnp.bfloat16),

time: 326 us -> 340 us (1.043)
  waiting for transfers between devices: 190 us -> 210 us
  matrix products: 80.7 us -> 73.6 us
    ppermute x0 -> x4, waiting for transfers between devices: none -> 173 us  [hidden_block(): lax.ppermute(summed, 'ctx', [(dev, dev ^ hop) for dev in range(4)])]
    psum x2 -> x0, waiting for transfers between devices: 153 us -> none  [hidden_block(): summed = lax.psum(partial_value, 'ctx')]
    dot_general x2, matrix products: 32.8 us -> 25.6 us  [hidden_block(): jnp.dot(hidden, w_down, preferred_element_type=jnp.float32)]
    another operation x2, other arithmetic: 4.17 us -> 0.5 us  [hidden_block(): partial_value = jnp.stack([gate_part, up_part], axis=1)]
  transfers between devices with their start and end apart: 5 -> 7, of which waited for: 5 -> 7; matrix products, arithmetic and copies ran while one was open for 0% -> 0% of each run, Pallas kernels for 0% -> 0%
where the time goes in v1:
time: 340 us; the launch traced here: 339 us
  waiting for transfers between devices  210 us (62%)
  matrix products  73.6 us (22%)
  blocking collectives  25.8 us (8%)
  between operations  13.6 us (4%)
  other arithmetic  10.4 us (3%)
  starting transfers between devices  3.92 us (1%)
    ppermute x4, waiting for transfers between devices, hidden_block(): lax.ppermute(summed, 'ctx', [(dev, dev ^ hop) for dev in range(4)])  173 us
    dot_general x2, matrix products, hidden_block(): jnp.dot(hidden, w_down, preferred_element_type=jnp.float32)  25.6 us
    dot_general x2, matrix products, hidden_block(): up_part = jnp.dot(row_piece, w_up, preferred_element_type=jnp.float32)  24 us
    dot_general x2, matrix products, hidden_block(): gate_part = jnp.dot(row_piece, w_gate, preferred_element_type=jnp.float32)  24 us
    reduce_scatter x2, waiting for transfers between devices, hidden_block(): lax.psum_scatter(jnp.dot(hidden, w_down, preferred_element_type=jnp.float...  22 us
    psum x2, blocking collectives, routed_layer(): squares, logits = lax.psum((squares, logits), 'ctx')  14 us
    ppermute x1, waiting for transfers between devices, from_behind(): return lax.ppermute(value, axis, pairs)  14 us
    all_gather x2, blocking collectives, hidden_block(): row_piece = lax.all_gather(normed, 'dp', axis=0, tiled=True)  11.7 us
  transfers between devices with their start and end apart: 7, of which 7 were waited for; matrix products, arithmetic and copies ran while one was open for 0% of the time, Pallas kernels for 0%

profile of v1, /device:TPU:0, one launch (start us, length us, event | category | flops | bytes accessed | tf_op | source)
XLA Modules:
  0.0 339.2 jit_solution(2210092652899768007)
XLA Ops:
  6.5 0.0 reduce-scatter.3.cloned.1.call-start
  6.5 1.0 copy.11
  7.6 0.7 compare_and_fusion
  8.3 0.7 compare_bitcast_fusion
  8.9 0.7 mul.113
  9.7 0.7 gather_fusion
  10.3 0.2 fusion.36
  10.5 8.3 %all-reduce.1 = (f32[32]{0:T(128)S(1)}, f32[32]{0:T(128)S(1)}) all-reduce(f32[32]{0:T(128)S(1)} %get-tuple-element.9, f32[32]{0:T(128)S(1)} %get-tuple-element.8), channel_id=1, replica_groups=mesh['section'=4,'ctx'=4,'dp'=2] {'ctx'}, use_global_device_ids=true, to_apply=%region_3.5 | all-reduce | flops 64 | bytes 512 | tf_op jit(solution)/shard_map/psum | solution.py:39
  18.9 0.8 fusion.40
  19.7 5.6 %all_gather.6 = bf16[64,2048]{1,0:T(8,128)(2,1)S(1)} all-gather(bf16[32,2048]{1,0:T(8,128)(2,1)S(1)} %fusion.40), channel_id=1, replica_groups=mesh['section'=4,'ctx'=4,'dp'=2] {'dp'}, dimensions={0}, use_global_device_ids=true | all-gather | bytes 393216 | tf_op jit(solution)/shard_map/all_gather | solution.py:17
  25.4 12.0 %fusion.12 = f32[64,1,7168]{2,0,1:T(8,128)S(1)} fusion(bf16[64,2048]{1,0:T(8,128)(2,1)S(1)} %all_gather.6, bf16[1,2048,7168]{2,1,0:T(8,128)(2,1)} %param.12), kind=kOutput, calls=%fused_computation.16 | convolution fusion | flops 1879048192 | bytes 31457280 | tf_op jit(solution)/shard_map/dot_general | solution.py:18
  37.3 12.0 %fusion.18 = f32[64,1,7168]{2,0,1:T(8,128)S(1)} fusion(bf16[64,2048]{1,0:T(8,128)(2,1)S(1)} %all_gather.6, bf16[1,2048,7168]{2,1,0:T(8,128)(2,1)} %param.13), kind=kOutput, calls=%fused_computation.18 | convolution fusion | flops 1879048192 | bytes 31457280 | tf_op jit(solution)/shard_map/dot_general | solution.py:19
  49.3 0.2 pad_maximum_fusion
  49.6 0.1 collective-permute-start
  49.7 6.4 %collective-permute-done = f32[64,2,7168]{2,0,1:T(8,128)S(1)} collective-permute-done((f32[64,2,7168]{2,0,1:T(8,128)S(1)}, f32[64,2,7168]{2,0,1:T(8,128)S(1)}, u32[]{:S(2)}, u32[]{:S(2)}) %collective-permute-start) | collective-permute-done | bytes 3670048 | tf_op jit(solution)/shard_map/ppermute | solution.py:23
  56.1 0.5 fusion.59
  56.6 0.7 collective-permute-start.1
  57.3 80.8 %collective-permute-done.1 = f32[64,2,7168]{2,0,1:T(8,128)S(1)} collective-permute-done((f32[64,2,7168]{2,0,1:T(8,128)S(1)}, f32[64,2,7168]{2,0,1:T(8,128)S(1)}, u32[]{:S(2)}, u32[]{:S(2)}) %collective-permute-start.1) | collective-permute-done | bytes 3670048 | tf_op jit(solution)/shard_map/ppermute | solution.py:23
  138.0 0.7 fusion.65
  138.7 0.0 copy-start.1
  138.7 0.0 copy-start
  138.8 12.8 %fusion.24 = bf16[64,2048]{1,0:T(8,128)(2,1)} fusion(bf16[1,7168,2048]{2,1,0:T(8,128)(2,1)} %param.14, f32[64,2,7168]{2,0,1:T(8,128)S(1)} %fusion.65), kind=kOutput, calls=%fused_computation.22 | convolution fusion | flops 1881931776 | bytes 33292288 | tf_op jit(solution)/shard_map/dot_general | solution.py:26
  151.6 0.0 reduce-scatter.3.cloned.1.call-update
  151.6 0.0 reduce-scatter.5.cloned.1.call-start
  151.7 0.0 copy-done.1
  151.7 12.1 %reduce-scatter.3.cloned.1.call-done = bf16[32,2048]{1,0:T(8,128)(2,1)} async-done(((bf16[64,2048]{1,0:T(8,128)(2,1)}), bf16[32,2048]{1,0:T(8,128)(2,1)}) %reduce-scatter.3.cloned.1.call-update) | async-done | bytes 131088 | tf_op jit(solution)/shard_map/reduce_scatter | solution.py:25
  163.8 1.6 scatter_custom_fusion
  165.3 1.5 collective-permute-start.2
  166.9 14.0 %collective-permute-done.2 = bf16[128,2048]{1,0:T(8,128)(2,1)S(1)} collective-permute-done((bf16[128,2048]{1,0:T(8,128)(2,1)S(1)}, bf16[128,2048]{1,0:T(8,128)(2,1)S(1)}, u32[]{:S(2)}, u32[]{:S(2)}) %collective-permute-start.2) | collective-permute-done | bytes 524320 | tf_op jit(solution)/shard_map/ppermute | solution.py:13
  180.9 0.6 gather_fusion.1
  181.5 0.2 fusion.42
  181.7 5.7 %all-reduce = (f32[32]{0:T(128)S(1)}, f32[32]{0:T(128)S(1)}) all-reduce(f32[32]{0:T(128)S(1)} %get-tuple-element.7, f32[32]{0:T(128)S(1)} %get-tuple-element.6), channel_id=1, replica_groups=mesh['section'=4,'ctx'=4,'dp'=2] {'ctx'}, use_global_device_ids=true, to_apply=%region_9.11 | all-reduce | flops 64 | bytes 512 | tf_op jit(solution)/shard_map/psum | solution.py:39
  187.4 0.0 copy-done
  187.4 0.1 fusion.46
  187.6 6.1 %all_gather.7 = bf16[64,2048]{1,0:T(8,128)(2,1)S(1)} all-gather(bf16[32,2048]{1,0:T(8,128)(2,1)S(1)} %fusion.46), channel_id=1, replica_groups=mesh['section'=4,'ctx'=4,'dp'=2] {'dp'}, dimensions={0}, use_global_device_ids=true | all-gather | bytes 393216 | tf_op jit(solution)/shard_map/all_gather | solution.py:17
  193.7 12.0 %fusion.15 = f32[64,1,7168]{2,0,1:T(8,128)S(1)} fusion(bf16[64,2048]{1,0:T(8,128)(2,1)S(1)} %all_gather.7, bf16[1,2048,7168]{2,1,0:T(8,128)(2,1)} %param.12), kind=kOutput, calls=%fused_computation.17 | convolution fusion | flops 1879048192 | bytes 31457280 | tf_op jit(solution)/shard_map/dot_general | solution.py:18
  205.7 12.0 %fusion.21 = f32[64,1,7168]{2,0,1:T(8,128)S(1)} fusion(bf16[64,2048]{1,0:T(8,128)(2,1)S(1)} %all_gather.7, bf16[1,2048,7168]{2,1,0:T(8,128)(2,1)} %param.13), kind=kOutput, calls=%fused_computation.19 | convolution fusion | flops 1879048192 | bytes 31457280 | tf_op jit(solution)/shard_map/dot_general | solution.py:19
  217.7 0.2 pad_maximum_fusion.1
  217.9 0.1 collective-permute-start.3
  218.0 6.4 %collective-permute-done.3 = f32[64,2,7168]{2,0,1:T(8,128)S(1)} collective-permute-done((f32[64,2,7168]{2,0,1:T(8,128)S(1)}, f32[64,2,7168]{2,0,1:T(8,128)S(1)}, u32[]{:S(2)}, u32[]{:S(2)}) %collective-permute-start.3) | collective-permute-done | bytes 3670048 | tf_op jit(solution)/shard_map/ppermute | solution.py:23
  224.4 0.5 fusion.58
  224.9 1.5 collective-permute-start.4
  226.4 79.9 %collective-permute-done.4 = f32[64,2,7168]{2,0,1:T(8,128)S(1)} collective-permute-done((f32[64,2,7168]{2,0,1:T(8,128)S(1)}, f32[64,2,7168]{2,0,1:T(8,128)S(1)}, u32[]{:S(2)}, u32[]{:S(2)}) %collective-permute-start.4) | collective-permute-done | bytes 3670048 | tf_op jit(solution)/shard_map/ppermute | solution.py:23
  306.4 0.7 fusion.64
  307.1 12.8 %fusion.27 = bf16[64,2048]{1,0:T(8,128)(2,1)} fusion(bf16[1,7168,2048]{2,1,0:T(8,128)(2,1)} %param.14, f32[64,2,7168]{2,0,1:T(8,128)S(1)} %fusion.64), kind=kOutput, calls=%fused_computation.23 | convolution fusion | flops 1881931776 | bytes 33292288 | tf_op jit(solution)/shard_map/dot_general | solution.py:26
  319.9 0.0 reduce-scatter.5.cloned.1.call-update
  320.0 9.9 %reduce-scatter.5.cloned.1.call-done = bf16[32,2048]{1,0:T(8,128)(2,1)} async-done(((bf16[64,2048]{1,0:T(8,128)(2,1)}), bf16[32,2048]{1,0:T(8,128)(2,1)}) %reduce-scatter.5.cloned.1.call-update) | async-done | bytes 131088 | tf_op jit(solution)/shard_map/reduce_scatter | solution.py:25
  329.9 1.6 scatter_custom_fusion.1
  331.5 0.9 select_bitcast_fusion
  (8 shorter events, 0.1 us)
Async XLA Ops:
  6.5 157.2 %reduce-scatter.3.cloned.1.call-start = ((), (), s32[]{:S(2)}) async-start(), calls=%async_computation.2 | async-start | bytes 393216 | tf_op jit(solution)/shard_map/reduce_scatter | solution.py:25
  49.6 6.5 %collective-permute-start = (f32[64,2,7168]{2,0,1:T(8,128)S(1)}, f32[64,2,7168]{2,0,1:T(8,128)S(1)}, u32[]{:S(2)}, u32[]{:S(2)}) collective-permute-start(f32[64,2,7168]{2,0,1:T(8,128)S(1)} %pad_maximum_fusion), channel_id=1, source_target_pairs={{0,2},{2,0},{4,6},{6,4},{1,3},{3,1},{5,7},{7,5},{8,10},{10,8},{12,... | collective-permute-start | bytes 11010056 | tf_op jit(solution)/shard_map/ppermute | solution.py:23
  56.6 81.4 %collective-permute-start.1 = (f32[64,2,7168]{2,0,1:T(8,128)S(1)}, f32[64,2,7168]{2,0,1:T(8,128)S(1)}, u32[]{:S(2)}, u32[]{:S(2)}) collective-permute-start(f32[64,2,7168]{2,0,1:T(8,128)S(1)} %fusion.59), channel_id=1, source_target_pairs={{0,4},{2,6},{4,0},{6,2},{1,5},{3,7},{5,1},{7,3},{8,12},{10,14},{12... | collective-permute-start | bytes 11010056 | tf_op jit(solution)/shard_map/ppermute | solution.py:23
  138.7 12.9 %copy-start.1 = (s32[2,1,1,32]{3,2,1,0:T(1,128)S(1)}, s32[2,1,1,32]{3,2,1,0:T(1,128)}, u32[]{:S(2)}) copy-start(s32[2,1,1,32]{3,2,1,0:T(1,128)} %param.15) | copy-start | bytes 772
  138.7 48.7 %copy-start = (f32[1,2048]{1,0:T(1,128)S(1)}, f32[1,2048]{1,0:T(1,128)}, u32[]{:S(2)}) copy-start(f32[1,2048]{1,0:T(1,128)} %param.10) | copy-start | bytes 24580
  151.6 178.3 %reduce-scatter.5.cloned.1.call-start = ((), (), s32[]{:S(2)}) async-start(), calls=%async_computation.3 | async-start | bytes 393216 | tf_op jit(solution)/shard_map/reduce_scatter | solution.py:25
  165.3 15.5 %collective-permute-start.2 = (bf16[128,2048]{1,0:T(8,128)(2,1)S(1)}, bf16[128,2048]{1,0:T(8,128)(2,1)S(1)}, u32[]{:S(2)}, u32[]{:S(2)}) collective-permute-start(bf16[128,2048]{1,0:T(8,128)(2,1)S(1)} %scatter_custom_fusion), channel_id=1, source_target_pairs={{0,8},{8,16},{16,24},{24,0},{1,9},{9,17},{17,25},{25,1},{2,10},{10... | collective-permute-start | bytes 1572872 | tf_op jit(solution)/shard_map/ppermute | solution.py:13
  217.9 6.5 %collective-permute-start.3 = (f32[64,2,7168]{2,0,1:T(8,128)S(1)}, f32[64,2,7168]{2,0,1:T(8,128)S(1)}, u32[]{:S(2)}, u32[]{:S(2)}) collective-permute-start(f32[64,2,7168]{2,0,1:T(8,128)S(1)} %pad_maximum_fusion.1), channel_id=1, source_target_pairs={{0,2},{2,0},{4,6},{6,4},{1,3},{3,1},{5,7},{7,5},{8,10},{10,8},{12,... | collective-permute-start | bytes 11010056 | tf_op jit(solution)/shard_map/ppermute | solution.py:23
  224.9 81.4 %collective-permute-start.4 = (f32[64,2,7168]{2,0,1:T(8,128)S(1)}, f32[64,2,7168]{2,0,1:T(8,128)S(1)}, u32[]{:S(2)}, u32[]{:S(2)}) collective-permute-start(f32[64,2,7168]{2,0,1:T(8,128)S(1)} %fusion.58), channel_id=1, source_target_pairs={{0,4},{2,6},{4,0},{6,2},{1,5},{3,7},{5,1},{7,3},{8,12},{10,14},{12... | collective-permute-start | bytes 11010056 | tf_op jit(solution)/shard_map/ppermute | solution.py:23
Sparse Core Ops, SparseCore 0:
  151.7 12.0 reduce-scatter.2
  320.0 9.8 reduce-scatter.4
